TPU v7x, 128 devices: a whole 4x4x4 slice. The times are simulated.
128 devices in a mesh: dp: 4 (over z_hi, core), dap: 32 (over y, z_lo, x).
Axes of the slice: x: 4, y: 4, z: 4 (z_hi: 2, z_lo: 2; z = z_hi * 2 + z_lo), core: 2. Of those that a mesh axis runs over, the one named last changes fastest.
Arguments:
- pair_in: bfloat16 [4, 256, 256, 128], P('dp', 'dap'), may hold values from -6 to 6
- residue_mask: int32 [4, 256], P('dp'), may hold values 0 or 1
- chain_index: int32 [4, 256], P('dp'), may hold values from 0 to 3, never falling along the last dimension, each value on 1 to 128 neighbouring positions
- chain_bias: float32 [128], replicated, may hold values from -3 to 3
- proj_weight: bfloat16 [2, 128, 640], replicated, may hold values from -0.5 to 0.5
- out_weight: bfloat16 [2, 128, 128], replicated, may hold values from -0.5 to 0.5
- cotangent: bfloat16 [4, 256, 256, 128], P('dp', 'dap'), may hold values from -6 to 6
Outputs:
- out_pair: bfloat16 [4, 256, 256, 128], P('dp', 'dap')
- pair_grad: bfloat16 [4, 256, 256, 128], P('dp', 'dap')
- grad_proj: float32 [2, 128, 640], replicated
- grad_out: float32 [2, 128, 128], replicated
- grad_chain: float32 [128], replicated
Inputs may be any that keep to these rules, and one draw needn't show every extreme that they name: `residue_mask`: 1 marks a residue that takes part, 0 one that is masked out. `chain_index`: chain numbers never fall along a complex; each chain holds 1 to 128 residues.
All inputs are finite; a program needn't handle non-finite values. No bound on the sum of `residue_mask` on one device may be relied on, other than what follows from the above.
Results may differ from a plain program's by a relative error of at most 0.028.
Values may be sent and summed in bfloat16 or wider, within the bound.
A program may use at most 128 MiB of HBM per device.

v0:
```python
import functools

import jax
import jax.numpy as jnp
from jax import lax
from jax.experimental import pallas as pl
from jax.experimental.pallas import tpu as pltpu
from jax.sharding import PartitionSpec as P

EPSILON = 1e-05
MESH = pl.DeviceIdType.MESH
F32 = jnp.float32
BF16 = jnp.bfloat16
ROWS = 8
CH = 128
BLOCK = 32

L1, R1, P1, L2, R2, P2, DP2, DL2, DR2, DP1, DL1, DR1 = range(12)


def nt(a, b):
    return lax.dot_general(a, b, (((1,), (1,)), ((), ())), preferred_element_type=F32)


def tn(a, b):
    return lax.dot_general(a, b, (((0,), (0,)), ((), ())), preferred_element_type=F32)


def nn(a, b):
    return jnp.dot(a, b, preferred_element_type=F32)


def one_hot(rows, columns, wanted):
    r = lax.broadcasted_iota(jnp.int32, (rows, columns), 0)
    q = lax.broadcasted_iota(jnp.int32, (rows, columns), 1)
    return jnp.where(wanted(r, q), 1.0, 0.0).astype(F32)


def sigmoid(x):
    return 0.5 * jnp.tanh(0.5 * x) + 0.5


def norm(x):
    centred = x - jnp.mean(x, axis=0, keepdims=True)
    inv = lax.rsqrt(jnp.mean(centred * centred, axis=0, keepdims=True) + EPSILON)
    return centred * inv, inv


def norm_back(normed, inv, g):
    first = jnp.mean(g, axis=0, keepdims=True)
    second = jnp.mean(g * normed, axis=0, keepdims=True)
    return (g - first - normed * second) * inv


def kernel(
    n, dp, pair_ref, mask_ref, chain_ref, bias_ref, pw_ref, ow_ref, cot_ref,
    out_ref, pg_ref, gproj_ref, gout_ref, gchain_ref,
    eye_s, eyek_s, pf_s, pt_s, pwt_s, owt_s, bias_s, pm_s, sc_s,
    z_s, cot_s, dz_s, nb_s, nrm_s, istd_s, side_s, gate_s, pn_s, pnb_s, pstd_s, upd_s,
    dupd_s, dproj_s, edge_s, in_s, mats_s, chain_s,
    send, recv, g_s, rs_s, dpx_s, dpr_s, red_s, ag_s,
    send_sem, recv_sem, gsend_sem, grecv_sem,
):
    width = n * ROWS
    group = CH // n
    rows = group * ROWS
    per = BLOCK * ROWS // rows
    blocks = CH // BLOCK
    me = lax.axis_index("dap")
    mine = lax.axis_index("dp")

    barrier = pltpu.get_barrier_semaphore()

    def greet(t, carry):
        pl.semaphore_signal(barrier, inc=1, device_id={"dap": lax.rem(me + t, n)}, device_id_type=MESH)
        return carry

    lax.fori_loop(1, n, greet, 0)

    def greet_dp(t, carry):
        pl.semaphore_signal(barrier, inc=1, device_id={"dp": lax.rem(mine + t, dp)}, device_id_type=MESH)
        return carry

    lax.fori_loop(1, dp, greet_dp, 0)

    eye_s[...] = one_hot(CH, CH, lambda r, q: r == q).astype(BF16)
    eyek_s[...] = one_hot(width, width, lambda r, q: r == q).astype(BF16)
    pf_s[...] = one_hot(256, 256, lambda r, q: q == (r % ROWS) * BLOCK + r // ROWS).astype(BF16)
    pt_s[...] = one_hot(256, 256, lambda r, q: q == (r % BLOCK) * ROWS + r // BLOCK).astype(BF16)
    diag = one_hot(CH, CH, lambda r, q: r == q)
    bias_s[...] = jnp.sum(diag * bias_ref[...], axis=1, keepdims=True)
    eye = eye_s[...]
    for t in range(2):
        for b in range(5):
            pwt_s[t, b * CH:(b + 1) * CH, :] = nt(eye, pw_ref[t, :, b * CH:(b + 1) * CH]).astype(BF16)
        owt_s[t] = nt(eye, ow_ref[t]).astype(BF16)
    live = mask_ref[...].astype(F32)
    chain = chain_ref[...].astype(F32)
    own = one_hot(ROWS, width, lambda r, q: q == r + ROWS * me)
    pm_s[...] = jnp.sum(own * live, axis=1, keepdims=True) * live
    sc_s[...] = jnp.where(jnp.sum(own * chain, axis=1, keepdims=True) == chain, 1.0, 0.0)

    def partner_of(t):
        y, z, x = me // 8, (me // 4) % 2, me % 4
        ny, nz, nx = (y + t // 8) % 4, (z + (t // 4) % 2) % 2, (x + t % 4) % 4
        return (ny * 2 + nz) * 4 + nx if n == 32 else (me + t) % n

    def start_exchange(a):
        recv[a, pl.ds(me, 1)] = send[a, pl.ds(me, 1)]

        def go(t, carry):
            to = partner_of((t * 11) % n)
            pltpu.make_async_remote_copy(
                src_ref=send.at[a, to], dst_ref=recv.at[a, me],
                send_sem=send_sem.at[a], recv_sem=recv_sem.at[a],
                device_id={"dap": to}, device_id_type=MESH,
            ).start()
            return carry

        lax.fori_loop(1, n, go, 0)

    def whole(a):
        return pltpu.make_async_remote_copy(
            src_ref=send.at[a, pl.ds(0, n - 1)], dst_ref=recv.at[a, pl.ds(0, n - 1)],
            send_sem=send_sem.at[a], recv_sem=recv_sem.at[a],
            device_id={"dap": lax.rem(me + 1, n)}, device_id_type=MESH,
        )

    def pack(a, e):
        def step(b, carry):
            x = edge_s[e, :, pl.ds(b * BLOCK, BLOCK), :].reshape(256, width)
            y = nn(pf_s[...], x).astype(BF16)
            send[a, pl.ds(b * per, per)] = y.reshape(per, rows, width)
            return carry

        lax.fori_loop(0, blocks, step, 0)

    def unpack(a, e):
        def step(b, carry):
            x = recv[a, pl.ds(b * per, per)].reshape(256, width)
            in_s[e, :, pl.ds(b * BLOCK, BLOCK), :] = nn(pt_s[...], x).reshape(ROWS, BLOCK, width)
            return carry

        lax.fori_loop(0, blocks, step, 0)

    def channel_pair(a, cp):
        x = recv[a, :, pl.ds(cp * 16, 16), :].astype(F32).reshape(n, 2, ROWS, width)
        return [x[:, h].reshape(width, width).astype(BF16) for h in range(2)]

    def send_pair(a, cp, items):
        x = jnp.concatenate([item.reshape(n, ROWS, width) for item in items], axis=1)
        send[a, :, pl.ds(cp * 16, 16), :] = x.astype(BF16)

    def triangle(t, la, ra, pa):
        def step(cp, carry):
            left, right = channel_pair(la, cp), channel_pair(ra, cp)
            items = []
            for h in range(2):
                mats_s[t, 0, 2 * cp + h] = left[h]
                mats_s[t, 1, 2 * cp + h] = right[h]
                items.append(nt(left[h], right[h]) if t == 0 else tn(left[h], right[h]))
            send_pair(pa, cp, items)
            return carry

        lax.fori_loop(0, group // 2, step, 0)

    def triangle_back(t, da, la, ra):
        def step(cp, carry):
            grads = channel_pair(da, cp)
            dl, dr = [], []
            for h in range(2):
                left, right = mats_s[t, 0, 2 * cp + h], mats_s[t, 1, 2 * cp + h]
                if t == 0:
                    dl.append(nn(grads[h], right))
                    dr.append(tn(grads[h], left))
                else:
                    dl.append(nt(right, grads[h]))
                    dr.append(nn(left, grads[h]))
            send_pair(la, cp, dl)
            send_pair(ra, cp, dr)
            return carry

        lax.fori_loop(0, group // 2, step, 0)

    def front(t, i, z):
        normed, inv = norm(z.astype(F32))
        nb = normed.astype(BF16)
        nrm_s[t, i], istd_s[t, i], nb_s[t, i] = normed, inv, nb
        pm = pm_s[pl.ds(i, 1), :]
        for e in range(2):
            value = nn(pwt_s[t, 2 * e * CH:(2 * e + 1) * CH, :], nb)
            scale = pm * sigmoid(nn(pwt_s[t, (2 * e + 1) * CH:(2 * e + 2) * CH, :], nb))
            edge = scale * value
            side_s[t, 2 * e, i] = scale
            side_s[t, 2 * e + 1, i] = edge
            edge_s[e, i] = edge.astype(BF16)

    def gates(t):
        def step(i, carry):
            gate_s[t, i] = sigmoid(nn(pwt_s[t, 4 * CH:5 * CH, :], nb_s[t, i]))
            return carry

        lax.fori_loop(0, ROWS, step, 0)

    def rear(t, i):
        normed, inv = norm(in_s[0, i])
        nb = normed.astype(BF16)
        update = nn(owt_s[t], nb)
        pn_s[t, i], pstd_s[t, i], pnb_s[t, i], upd_s[t, i] = normed, inv, nb, update
        return (z_s[t, i].astype(F32) + gate_s[t, i] * update).astype(BF16)

    def rear_back(t, i, up):
        gate = gate_s[t, i]
        dupd = (up * gate).astype(BF16)
        dupd_s[i] = dupd
        dproj_s[4, i] = (up * upd_s[t, i] * gate * (1.0 - gate)).astype(BF16)
        g = nn(ow_ref[t], dupd)
        edge_s[0, i] = norm_back(pn_s[t, i], pstd_s[t, i], g).astype(BF16)

    def front_back(t, i, up):
        h = nn(pw_ref[t, :, 4 * CH:5 * CH], dproj_s[4, i])
        for e in range(2):
            grad, scale = in_s[e, i], side_s[t, 2 * e, i]
            first = (grad * scale).astype(BF16)
            second = (grad * side_s[t, 2 * e + 1, i] * (1.0 - scale)).astype(BF16)
            dproj_s[2 * e, i], dproj_s[2 * e + 1, i] = first, second
            h += nn(pw_ref[t, :, 2 * e * CH:(2 * e + 1) * CH], first)
            h += nn(pw_ref[t, :, (2 * e + 1) * CH:(2 * e + 2) * CH], second)
        return (up + norm_back(nrm_s[t, i], istd_s[t, i], h)).astype(BF16)

    def put_grad(t, b, value):
        g_rows = CH * 6 // n
        if CH % g_rows == 0:
            count = CH // g_rows
            g_s[t, b * count:(b + 1) * count, 0:g_rows, :] = value.reshape(count, g_rows, CH)
        else:
            at = b * CH
            done = 0
            while done < CH:
                piece, offset = divmod(at + done, g_rows)
                size = min(g_rows - offset, CH - done)
                g_s[t, piece, offset:offset + size, :] = value[done:done + size]
                done += size

    def out_grad(t):
        total = nt(pnb_s[t, 0], dupd_s[0])
        for i in range(1, ROWS):
            total += nt(pnb_s[t, i], dupd_s[i])
        put_grad(t, 5, total)

    def proj_grad(t, b):
        total = nt(nb_s[t, 0], dproj_s[b, 0])
        for i in range(1, ROWS):
            total += nt(nb_s[t, i], dproj_s[b, i])
        put_grad(t, b, total)

    def start_scatter(t):
        rs_s[t, pl.ds(me, 1)] = g_s[t, pl.ds(me, 1)]

        def go(k, carry):
            to = partner_of((k * 11) % n)
            pltpu.make_async_remote_copy(
                src_ref=g_s.at[t, to], dst_ref=rs_s.at[t, me],
                send_sem=gsend_sem.at[t, 0], recv_sem=grecv_sem.at[t, 0],
                device_id={"dap": to}, device_id_type=MESH,
            ).start()
            return carry

        lax.fori_loop(1, n, go, 0)

    def whole_scatter(t):
        return pltpu.make_async_remote_copy(
            src_ref=g_s.at[t, pl.ds(0, n - 1)], dst_ref=rs_s.at[t, pl.ds(0, n - 1)],
            send_sem=gsend_sem.at[t, 0], recv_sem=grecv_sem.at[t, 0],
            device_id={"dap": lax.rem(me + 1, n)}, device_id_type=MESH,
        )

    def start_across(t):
        whole_scatter(t).wait_recv()
        total = rs_s[t, 0]
        for k in range(1, n):
            total += rs_s[t, k]
        dpx_s[t] = total
        dpr_s[t, mine] = total

        def go(k, carry):
            pltpu.make_async_remote_copy(
                src_ref=dpx_s.at[t], dst_ref=dpr_s.at[t, mine],
                send_sem=gsend_sem.at[t, 1], recv_sem=grecv_sem.at[t, 1],
                device_id={"dp": lax.rem(mine + k, dp)}, device_id_type=MESH,
            ).start()
            return carry

        lax.fori_loop(1, dp, go, 0)

    def whole_across(t):
        return pltpu.make_async_remote_copy(
            src_ref=dpr_s.at[t, pl.ds(0, dp - 1)], dst_ref=dpr_s.at[t, pl.ds(0, dp - 1)],
            send_sem=gsend_sem.at[t, 1], recv_sem=grecv_sem.at[t, 1],
            device_id={"dp": lax.rem(mine + 1, dp)}, device_id_type=MESH,
        )

    def start_gather(t):
        whole_across(t).wait_recv()
        total = dpr_s[t, 0]
        for k in range(1, dp):
            total += dpr_s[t, k]
        total = total * (1.0 / (dp * width))
        red_s[t] = total
        ag_s[t, me] = total

        def go(k, carry):
            to = partner_of((k * 11) % n)
            pltpu.make_async_remote_copy(
                src_ref=red_s.at[t], dst_ref=ag_s.at[t, me],
                send_sem=gsend_sem.at[t, 2], recv_sem=grecv_sem.at[t, 2],
                device_id={"dap": to}, device_id_type=MESH,
            ).start()
            return carry

        lax.fori_loop(1, n, go, 0)

    def whole_gather(t):
        return pltpu.make_async_remote_copy(
            src_ref=ag_s.at[t, pl.ds(0, n - 1)], dst_ref=ag_s.at[t, pl.ds(0, n - 1)],
            send_sem=gsend_sem.at[t, 2], recv_sem=grecv_sem.at[t, 2],
            device_id={"dap": lax.rem(me + 1, n)}, device_id_type=MESH,
        )

    def finish_grad(t):
        whole_gather(t).wait_recv()
        g_rows = CH * 6 // n
        full = ag_s[t][:, 0:g_rows, :].reshape(6 * CH, CH)
        for b in range(5):
            gproj_ref[t, :, b * CH:(b + 1) * CH] = full[b * CH:(b + 1) * CH]
        gout_ref[t] = full[5 * CH:]

    def loop(body):
        def step(i, carry):
            body(i)
            return carry

        lax.fori_loop(0, ROWS, step, 0)

    def begin(i):
        x = nt(eye_s[...], pair_ref[i])
        z = (x + sc_s[pl.ds(i, 1), :] * bias_s[...]).astype(BF16)
        z_s[0, i] = z
        front(0, i, z)

    loop(begin)
    pack(L1, 0)
    pl.semaphore_wait(barrier, n - 1 + dp - 1)
    start_exchange(L1)
    pack(R1, 1)
    start_exchange(R1)
    gates(0)

    def turn(i):
        cot_s[i] = nt(eye_s[...], cot_ref[i]).astype(BF16)

    loop(turn)
    whole(L1).wait_recv()
    whole(R1).wait_recv()
    triangle(0, L1, R1, P1)
    start_exchange(P1)
    whole(P1).wait_recv()
    unpack(P1, 0)

    def middle(i):
        z = rear(0, i)
        z_s[1, i] = z
        front(1, i, z)

    loop(middle)
    pack(L2, 0)
    start_exchange(L2)
    pack(R2, 1)
    start_exchange(R2)
    gates(1)
    whole(L2).wait_recv()
    whole(R2).wait_recv()
    triangle(1, L2, R2, P2)
    start_exchange(P2)
    whole(P2).wait_recv()
    unpack(P2, 0)

    def last(i):
        z_s[2, i] = rear(1, i)
        rear_back(1, i, cot_s[i].astype(F32))

    loop(last)
    pack(DP2, 0)
    start_exchange(DP2)

    def write_out(i):
        out_ref[i] = nt(eyek_s[...], z_s[2, i]).astype(BF16)

    loop(write_out)
    out_grad(1)
    whole(DP2).wait_recv()
    triangle_back(1, DP2, DL2, DR2)
    start_exchange(DL2)
    start_exchange(DR2)
    whole(DL2).wait_recv()
    unpack(DL2, 0)
    whole(DR2).wait_recv()
    unpack(DR2, 1)

    def back(i):
        dz_s[0, i] = front_back(1, i, cot_s[i].astype(F32))

    loop(back)
    for b in range(5):
        proj_grad(1, b)
    g_s[1, :, CH * 6 // n:, :] = jnp.zeros((n, 8, CH), F32)

    def again(i):
        rear_back(0, i, dz_s[0, i].astype(F32))

    loop(again)
    pack(DP1, 0)
    start_exchange(DP1)
    start_scatter(1)
    out_grad(0)
    whole(DP1).wait_recv()
    triangle_back(0, DP1, DL1, DR1)
    start_exchange(DL1)
    start_exchange(DR1)
    start_across(1)
    start_gather(1)
    whole(DL1).wait_recv()
    unpack(DL1, 0)
    whole(DR1).wait_recv()
    unpack(DR1, 1)
    chain_s[...] = jnp.zeros_like(chain_s)

    def end(i):
        grad = front_back(0, i, dz_s[0, i].astype(F32))
        dz_s[1, i] = grad
        chain_s[...] += grad.astype(F32) * sc_s[pl.ds(i, 1), :]

    loop(end)
    for b in range(5):
        proj_grad(0, b)
    column = jnp.sum(chain_s[...], axis=1, keepdims=True)
    row = jnp.sum(diag * column, axis=0, keepdims=True)
    g_s[0, :, CH * 6 // n:, :] = jnp.broadcast_to(row[None], (n, 8, CH))
    start_scatter(0)

    def write_grad(i):
        pg_ref[i] = nt(eyek_s[...], dz_s[1, i]).astype(BF16)

    loop(write_grad)
    finish_grad(1)
    start_across(0)
    start_gather(0)
    gchain_ref[...] = red_s[0, CH * 6 // n:CH * 6 // n + 1, :]
    finish_grad(0)

    def drain(a, carry):
        whole(a).wait_send()
        return carry

    lax.fori_loop(0, 12, drain, 0)
    for t in range(2):
        whole_scatter(t).wait_send()
        whole_across(t).wait_send()
        whole_gather(t).wait_send()


def body(n, dp, pair_in, residue_mask, chain_index, chain_bias, proj_weight, out_weight, cotangent):
    width = n * ROWS
    group = CH // n
    grad_rows = CH * 6 // n + 8
    tensor = (ROWS, CH, width)
    vmem = pl.BlockSpec(memory_space=pltpu.VMEM)
    shapes = [
        jax.ShapeDtypeStruct((ROWS, width, CH), BF16),
        jax.ShapeDtypeStruct((ROWS, width, CH), BF16),
        jax.ShapeDtypeStruct((2, CH, 5 * CH), F32),
        jax.ShapeDtypeStruct((2, CH, CH), F32),
        jax.ShapeDtypeStruct((1, CH), F32),
    ]
    scratch = [
        pltpu.VMEM((CH, CH), BF16),
        pltpu.VMEM((width, width), BF16),
        pltpu.VMEM((256, 256), BF16),
        pltpu.VMEM((256, 256), BF16),
        pltpu.VMEM((2, 5 * CH, CH), BF16),
        pltpu.VMEM((2, CH, CH), BF16),
        pltpu.VMEM((CH, 1), F32),
        pltpu.VMEM((ROWS, width), F32),
        pltpu.VMEM((ROWS, width), F32),
        pltpu.VMEM((3,) + tensor, BF16),
        pltpu.VMEM(tensor, BF16),
        pltpu.VMEM((2,) + tensor, BF16),
        pltpu.VMEM((2,) + tensor, BF16),
        pltpu.VMEM((2,) + tensor, F32),
        pltpu.VMEM((2, ROWS, 1, width), F32),
        pltpu.VMEM((2, 4) + tensor, F32),
        pltpu.VMEM((2,) + tensor, F32),
        pltpu.VMEM((2,) + tensor, F32),
        pltpu.VMEM((2,) + tensor, BF16),
        pltpu.VMEM((2, ROWS, 1, width), F32),
        pltpu.VMEM((2,) + tensor, F32),
        pltpu.VMEM(tensor, BF16),
        pltpu.VMEM((5,) + tensor, BF16),
        pltpu.VMEM((2,) + tensor, BF16),
        pltpu.VMEM((2,) + tensor, F32),
        pltpu.VMEM((2, 2, group, width, width), BF16),
        pltpu.VMEM((CH, width), F32),
        pltpu.VMEM((12, n, group * ROWS, width), BF16),
        pltpu.VMEM((12, n, group * ROWS, width), BF16),
        pltpu.VMEM((2, n, grad_rows, CH), F32),
        pltpu.VMEM((2, n, grad_rows, CH), F32),
        pltpu.VMEM((2, grad_rows, CH), F32),
        pltpu.VMEM((2, dp, grad_rows, CH), F32),
        pltpu.VMEM((2, grad_rows, CH), F32),
        pltpu.VMEM((2, n, grad_rows, CH), F32),
        pltpu.SemaphoreType.DMA((12,)),
        pltpu.SemaphoreType.DMA((12,)),
        pltpu.SemaphoreType.DMA((2, 3)),
        pltpu.SemaphoreType.DMA((2, 3)),
    ]
    out_pair, pair_grad, grad_proj, grad_out, grad_chain = pl.pallas_call(
        functools.partial(kernel, n, dp),
        out_shape=shapes,
        in_specs=[vmem] * 7,
        out_specs=[vmem] * 5,
        scratch_shapes=scratch,
        compiler_params=pltpu.CompilerParams(
            collective_id=0, has_side_effects=True, vmem_limit_bytes=60 * 1024 * 1024
        ),
    )(
        pair_in[0], residue_mask, chain_index, chain_bias.reshape(1, CH),
        proj_weight, out_weight, cotangent[0],
    )
    return out_pair[None], pair_grad[None], grad_proj, grad_out, grad_chain.reshape(CH)


def solution(mesh):
    n, dp = mesh.shape["dap"], mesh.shape["dp"]
    rows = P("dp", "dap", None, None)
    return jax.shard_map(
        functools.partial(body, n, dp),
        mesh=mesh,
        in_specs=(rows, P("dp", None), P("dp", None), P(), P(), P(), rows),
        out_specs=(rows, rows, P(), P(), P()),
        check_vma=False,
    )
```

profile of v0, /device:TPU:1, one launch (start us, length us, event | category | flops | bytes accessed | tf_op | source)
XLA Modules:
  0.0 152.3 jit_solution(14146560890531181422)
XLA Ops:
  0.6 146.3 %shard_map.110 = (bf16[8,256,128]{2,1,0:T(8,128)(2,1)}, bf16[8,256,128]{2,1,0:T(8,128)(2,1)}, f32[2,128,640]{2,1,0:T(8,128)}, f32[2,128,128]{2,1,0:T(8,128)}, f32[1,128]{1,0:T(1,128)}) custom-call(bf16[8,256,128]{2,1,0:T(8,128)(2,1)} %bitcast.8, s32[1,256]{1,0:T(1,128)} %mask_ref.1, s32[1,256]{1,0:T(1,128)} %chain_ref.1, f32[1,128]{1,0:T(1,128)} %bitcast.10, ...), custom_call_target="tpu_custom_call" | custom-call | tf_op jit(solution)/shard_map/pallas_call | solution.py:526
  146.9 0.0 copy-start.1
  146.9 1.9 %copy.17 = bf16[1,8,256,128]{3,2,1,0:T(8,128)(2,1)} copy(bf16[1,8,256,128]{3,2,1,0:T(8,128)(2,1)} %bitcast.7) | data formatting | bytes 1048576
  148.8 0.0 copy-done.1
  148.9 0.0 copy-start
  148.9 0.8 copy.18
  149.6 0.5 copy-done
  150.1 0.0 copy-start.2
  150.1 0.8 copy.19
  151.0 0.2 copy-done.2
  151.2 0.0 copy-start.3
  151.2 0.7 copy.20
  151.8 0.0 copy-done.3
  151.8 0.5 copy.21
Async XLA Ops:
  146.9 1.9 %copy-start.1 = (bf16[8,256,128]{2,1,0:T(8,128)(2,1)S(1)}, bf16[8,256,128]{2,1,0:T(8,128)(2,1)}, u32[]{:S(2)}) copy-start(bf16[8,256,128]{2,1,0:T(8,128)(2,1)} %get-tuple-element.11) | copy-start | bytes 1572868
  148.9 1.3 copy-start
  150.1 1.0 copy-start.2
  151.2 0.7 copy-start.3
where the time goes:
time: 153 us; the launch traced here: 152 us
  Pallas kernels  146 us (95%)
  local copies, waits for them, and re-layouts  5.4 us (4%)
    pallas_call x1, Pallas kernels, body(): pl.pallas_call(functools.partial(kernel, n, dp), out_shape=shapes, in_spe...  146 us
    unnamed x13, local copies, waits for them, and re-layouts  5.4 us

commit v1 on v0

v1 whole, which is shorter than its diff:
```python
import functools

import jax
import jax.numpy as jnp
from jax import lax
from jax.experimental import pallas as pl
from jax.experimental.pallas import tpu as pltpu
from jax.sharding import PartitionSpec as P

EPSILON = 1e-05
MESH = pl.DeviceIdType.MESH
F32 = jnp.float32
BF16 = jnp.bfloat16
ROWS = 8
CH = 128
BLOCK = 32

L1, R1, P1, L2, R2, P2, DP2, DL2, DR2, DP1, DL1, DR1 = range(12)


def nt(a, b):
    return lax.dot_general(a, b, (((1,), (1,)), ((), ())), preferred_element_type=F32)


def tn(a, b):
    return lax.dot_general(a, b, (((0,), (0,)), ((), ())), preferred_element_type=F32)


def nn(a, b):
    return jnp.dot(a, b, preferred_element_type=F32)


def one_hot(rows, columns, wanted):
    r = lax.broadcasted_iota(jnp.int32, (rows, columns), 0)
    q = lax.broadcasted_iota(jnp.int32, (rows, columns), 1)
    return jnp.where(wanted(r, q), 1.0, 0.0).astype(F32)


def sigmoid(x):
    return 0.5 * jnp.tanh(0.5 * x) + 0.5


def norm(x):
    centred = x - jnp.mean(x, axis=0, keepdims=True)
    inv = lax.rsqrt(jnp.mean(centred * centred, axis=0, keepdims=True) + EPSILON)
    return centred * inv, inv


def norm_back(normed, inv, g):
    first = jnp.mean(g, axis=0, keepdims=True)
    second = jnp.mean(g * normed, axis=0, keepdims=True)
    return (g - first - normed * second) * inv


def kernel(
    n, dp, pair_ref, mask_ref, chain_ref, bias_ref, pw_ref, ow_ref, cot_ref,
    out_ref, pg_ref, gproj_ref, gout_ref, gchain_ref,
    eye_s, pf_s, pt_s, pwt_s, owt_s, bias_s, pm_s, sc_s,
    z_s, cot_s, dz_s, nb_s, nrm_s, istd_s, side_s, gate_s, pn_s, pnb_s, pstd_s, upd_s,
    dupd_s, dproj_s, edge_s, in_s, mats_s, chain_s, acc_s,
    send, recv, ge_s, re_s, ae_s, gf_s, rf_s, af_s, xe_s, ye_s, xf_s, yf_s, cg_s, cr_s, cx_s, cy_s,
    send_sem, recv_sem, gsend_sem, grecv_sem,
):
    width = n * ROWS
    half = width // 2
    group = CH // n
    rows = group * ROWS
    half_rows = rows // 2
    per = BLOCK * ROWS // rows
    blocks = CH // BLOCK
    me = lax.axis_index("dap")
    mine = lax.axis_index("dp")

    barrier = pltpu.get_barrier_semaphore()

    def greet(t, carry):
        pl.semaphore_signal(barrier, inc=1, device_id={"dap": lax.rem(me + t, n)}, device_id_type=MESH)
        return carry

    lax.fori_loop(1, n, greet, 0)

    def greet_dp(t, carry):
        pl.semaphore_signal(barrier, inc=1, device_id={"dp": lax.rem(mine + t, dp)}, device_id_type=MESH)
        return carry

    lax.fori_loop(1, dp, greet_dp, 0)

    eye_s[...] = one_hot(CH, CH, lambda r, q: r == q).astype(BF16)
    pf_s[...] = one_hot(256, 256, lambda r, q: q == (r % ROWS) * BLOCK + r // ROWS).astype(BF16)
    pt_s[...] = one_hot(256, 256, lambda r, q: q == (r % BLOCK) * ROWS + r // BLOCK).astype(BF16)
    diag = one_hot(CH, CH, lambda r, q: r == q)
    bias_s[...] = jnp.sum(diag * bias_ref[...], axis=1, keepdims=True)
    eye = eye_s[...]
    for t in range(2):
        for b in range(5):
            pwt_s[t, b * CH:(b + 1) * CH, :] = nt(eye, pw_ref[t, :, b * CH:(b + 1) * CH]).astype(BF16)
        owt_s[t] = nt(eye, ow_ref[t]).astype(BF16)
    live = mask_ref[...].astype(F32)
    chain = chain_ref[...].astype(F32)
    own = one_hot(ROWS, width, lambda r, q: q == r + ROWS * me)
    pair_mask = jnp.sum(own * live, axis=1, keepdims=True) * live
    same = jnp.where(jnp.sum(own * chain, axis=1, keepdims=True) == chain, 1.0, 0.0)
    for p in range(2):
        pm_s[p * ROWS:(p + 1) * ROWS, :] = pair_mask[:, p * half:(p + 1) * half]
        sc_s[p * ROWS:(p + 1) * ROWS, :] = same[:, p * half:(p + 1) * half]

    def partner_of(t):
        y, z, x = me // 8, (me // 4) % 2, me % 4
        ny, nz, nx = (y + t // 8) % 4, (z + (t // 4) % 2) % 2, (x + t % 4) % 4
        return (ny * 2 + nz) * 4 + nx if n == 32 else (me + t) % n

    def push(messages):
        for a, r0, rn, p, k in messages:
            at = (a, pl.ds(me, 1), slice(r0, r0 + rn), slice(p * half, (p + 1) * half))
            recv[at] = send[at]

        def go(t, carry):
            to = partner_of((t * 11) % n)
            for a, r0, rn, p, k in messages:
                part = (pl.ds(r0, rn), pl.ds(p * half, half))
                pltpu.make_async_remote_copy(
                    src_ref=send.at[(a, to) + part], dst_ref=recv.at[(a, me) + part],
                    send_sem=send_sem.at[a], recv_sem=recv_sem.at[a, k],
                    device_id={"dap": to}, device_id_type=MESH,
                ).start()
            return carry

        lax.fori_loop(1, n, go, 0)

    def arrived(a, r0, rn, p, k):
        part = (a, pl.ds(0, n - 1), pl.ds(r0, rn), pl.ds(p * half, half))
        pltpu.make_async_remote_copy(
            src_ref=send.at[part], dst_ref=recv.at[part],
            send_sem=send_sem.at[a], recv_sem=recv_sem.at[a, k],
            device_id={"dap": lax.rem(me + 1, n)}, device_id_type=MESH,
        ).wait_recv()

    def sent(a):
        part = (a, pl.ds(0, n - 1))
        pltpu.make_async_remote_copy(
            src_ref=send.at[part], dst_ref=recv.at[part],
            send_sem=send_sem.at[a], recv_sem=recv_sem.at[a, 0],
            device_id={"dap": lax.rem(me + 1, n)}, device_id_type=MESH,
        ).wait_send()

    def to_channels(p, items):
        if p == 0:
            push([(a, 0, rows, 0, 0) for a in items])
        else:
            push([(a, 0, half_rows, 1, 1) for a in items])
            push([(a, half_rows, half_rows, 1, 2) for a in items])

    def channels_here(cc, items):
        for a in items:
            if cc == 0:
                arrived(a, 0, rows, 0, 0)
            arrived(a, cc * half_rows, half_rows, 1, 1 + cc)

    def to_pairs(cc, items):
        push([(a, cc * half_rows, half_rows, 0, 0) for a in items])
        if cc == 1:
            push([(a, 0, rows, 1, 1) for a in items])

    def pairs_here(p, a):
        arrived(a, 0, rows, p, p)

    def pack(p, a, e):
        def step(b, carry):
            x = edge_s[e, p * ROWS:(p + 1) * ROWS, pl.ds(b * BLOCK, BLOCK), :].reshape(256, half)
            y = nn(pf_s[...], x).astype(BF16)
            send[a, pl.ds(b * per, per), :, p * half:(p + 1) * half] = y.reshape(per, rows, half)
            return carry

        lax.fori_loop(0, blocks, step, 0, unroll=4)

    def unpack(p, a, e):
        def step(b, carry):
            x = recv[a, pl.ds(b * per, per), :, p * half:(p + 1) * half].reshape(256, half)
            y = nn(pt_s[...], x).reshape(ROWS, BLOCK, half)
            in_s[e, p * ROWS:(p + 1) * ROWS, pl.ds(b * BLOCK, BLOCK), :] = y
            return carry

        lax.fori_loop(0, blocks, step, 0, unroll=4)

    def channel_pair(a, at):
        x = recv[a, :, at:at + 16, :].astype(F32).reshape(n, 2, ROWS, width)
        return [x[:, h].reshape(width, width).astype(BF16) for h in range(2)]

    def put_pair(a, at, items):
        x = jnp.concatenate([item.reshape(n, ROWS, width) for item in items], axis=1)
        send[a, :, at:at + 16, :] = x.astype(BF16)

    def triangle(t, la, ra, pa):
        for cc in range(2):
            channels_here(cc, (la, ra))
            for cp in range(cc * group // 4, (cc + 1) * group // 4):
                left, right = channel_pair(la, cp * 16), channel_pair(ra, cp * 16)
                items = []
                for h in range(2):
                    mats_s[t, 0, 2 * cp + h] = left[h]
                    mats_s[t, 1, 2 * cp + h] = right[h]
                    items.append(nt(left[h], right[h]) if t == 0 else tn(left[h], right[h]))
                put_pair(pa, cp * 16, items)
            to_pairs(cc, (pa,))

    def triangle_back(t, da, la, ra):
        for cc in range(2):
            channels_here(cc, (da,))
            for cp in range(cc * group // 4, (cc + 1) * group // 4):
                grads = channel_pair(da, cp * 16)
                dl, dr = [], []
                for h in range(2):
                    left, right = mats_s[t, 0, 2 * cp + h], mats_s[t, 1, 2 * cp + h]
                    if t == 0:
                        dl.append(nn(grads[h], right))
                        dr.append(tn(grads[h], left))
                    else:
                        dl.append(nt(right, grads[h]))
                        dr.append(nn(left, grads[h]))
                put_pair(la, cp * 16, dl)
                put_pair(ra, cp * 16, dr)
            to_pairs(cc, (la, ra))

    def front(t, q, z):
        normed, inv = norm(z.astype(F32))
        nb = normed.astype(BF16)
        nrm_s[t, q], istd_s[t, q], nb_s[t, q] = normed, inv, nb
        pm = pm_s[pl.ds(q, 1), :]
        for e in range(2):
            value = nn(pwt_s[t, 2 * e * CH:(2 * e + 1) * CH, :], nb)
            scale = pm * sigmoid(nn(pwt_s[t, (2 * e + 1) * CH:(2 * e + 2) * CH, :], nb))
            edge = scale * value
            side_s[t, 2 * e, q] = scale
            side_s[t, 2 * e + 1, q] = edge
            edge_s[e, q] = edge.astype(BF16)

    def gates(t):
        def step(q, carry):
            gate_s[t, q] = sigmoid(nn(pwt_s[t, 4 * CH:5 * CH, :], nb_s[t, q]))
            return carry

        lax.fori_loop(0, 2 * ROWS, step, 0, unroll=8)

    def rear(t, q):
        normed, inv = norm(in_s[0, q])
        nb = normed.astype(BF16)
        update = nn(owt_s[t], nb)
        pn_s[t, q], pstd_s[t, q], pnb_s[t, q], upd_s[t, q] = normed, inv, nb, update
        return (z_s[t, q].astype(F32) + gate_s[t, q] * update).astype(BF16)

    def rear_back(t, q, up):
        gate = gate_s[t, q]
        dupd = (up * gate).astype(BF16)
        dupd_s[t, q] = dupd
        dproj_s[t, 4, q] = (up * upd_s[t, q] * gate * (1.0 - gate)).astype(BF16)
        g = nn(ow_ref[t], dupd)
        edge_s[0, q] = norm_back(pn_s[t, q], pstd_s[t, q], g).astype(BF16)

    def front_back(t, q, up):
        h = nn(pw_ref[t, :, 4 * CH:5 * CH], dproj_s[t, 4, q])
        for e in range(2):
            grad, scale = in_s[e, q], side_s[t, 2 * e, q]
            first = (grad * scale).astype(BF16)
            second = (grad * side_s[t, 2 * e + 1, q] * (1.0 - scale)).astype(BF16)
            dproj_s[t, 2 * e, q], dproj_s[t, 2 * e + 1, q] = first, second
            h += nn(pw_ref[t, :, 2 * e * CH:(2 * e + 1) * CH], first)
            h += nn(pw_ref[t, :, (2 * e + 1) * CH:(2 * e + 2) * CH], second)
        return (up + norm_back(nrm_s[t, q], istd_s[t, q], h)).astype(BF16)

    early_rows, late_rows = 8 * CH // n, 4 * CH // n

    def out_grad(t):
        total = nt(pnb_s[t, 0], dupd_s[t, 0])
        for q in range(1, 2 * ROWS):
            total += nt(pnb_s[t, q], dupd_s[t, q])
        return total

    def proj_grad(t, b, p=None):
        first, last = (0, 2 * ROWS) if p is None else (p * ROWS, (p + 1) * ROWS)
        total = nt(nb_s[t, first], dproj_s[t, b, first])
        for q in range(first + 1, last):
            total += nt(nb_s[t, q], dproj_s[t, b, q])
        return total

    def piece(at, size):
        return pl.ds(pl.multiple_of(at * size, size), size)

    def scatter(g, r, size, k):
        r[pl.ds(me, 1)] = g[piece(me, size), :].reshape(1, size, CH)

        def go(t, carry):
            to = partner_of((t * 11) % n)
            pltpu.make_async_remote_copy(
                src_ref=g.at[piece(to, size)], dst_ref=r.at[me],
                send_sem=gsend_sem.at[k], recv_sem=grecv_sem.at[k],
                device_id={"dap": to}, device_id_type=MESH,
            ).start()
            return carry

        lax.fori_loop(1, n, go, 0)

    def spread(x, r, k):
        def go(t, carry):
            to = partner_of((t * 11) % n)
            pltpu.make_async_remote_copy(
                src_ref=x, dst_ref=r.at[me], send_sem=gsend_sem.at[k], recv_sem=grecv_sem.at[k],
                device_id={"dap": to}, device_id_type=MESH,
            ).start()
            return carry

        lax.fori_loop(1, n, go, 0)

    def across(x, y, k):
        y[mine] = x[...]

        def go(t, carry):
            pltpu.make_async_remote_copy(
                src_ref=x, dst_ref=y.at[mine], send_sem=gsend_sem.at[k], recv_sem=grecv_sem.at[k],
                device_id={"dp": lax.rem(mine + t, dp)}, device_id_type=MESH,
            ).start()
            return carry

        lax.fori_loop(1, dp, go, 0)

    def bulk(r, count, k):
        return pltpu.make_async_remote_copy(
            src_ref=r.at[pl.ds(0, count)], dst_ref=r.at[pl.ds(0, count)],
            send_sem=gsend_sem.at[k], recv_sem=grecv_sem.at[k],
            device_id={"dap": lax.rem(me + 1, n)}, device_id_type=MESH,
        )

    def summed(r, count):
        total = r[0].astype(F32)
        for t in range(1, count):
            total += r[t].astype(F32)
        return total

    inverse = 1.0 / (dp * width)

    def loop(body, p):
        def step(i, carry):
            body(i, i + p * ROWS)
            return carry

        lax.fori_loop(0, ROWS, step, 0, unroll=8)

    for p in range(2):
        def begin(i, q):
            x = nt(eye_s[...], pair_ref[i, p * half:(p + 1) * half, :])
            z = (x + sc_s[pl.ds(q, 1), :] * bias_s[...]).astype(BF16)
            z_s[0, q] = z
            front(0, q, z)

        loop(begin, p)
        pack(p, L1, 0)
        pack(p, R1, 1)
        if p == 0:
            pl.semaphore_wait(barrier, n - 1 + dp - 1)
        to_channels(p, (L1, R1))
    gates(0)
    for p in range(2):
        def turn(i, q):
            cot_s[q] = nt(eye_s[...], cot_ref[i, p * half:(p + 1) * half, :]).astype(BF16)

        loop(turn, p)
    triangle(0, L1, R1, P1)
    for p in range(2):
        def middle(i, q):
            z = rear(0, q)
            z_s[1, q] = z
            front(1, q, z)

        pairs_here(p, P1)
        unpack(p, P1, 0)
        loop(middle, p)
        pack(p, L2, 0)
        pack(p, R2, 1)
        to_channels(p, (L2, R2))
    gates(1)
    triangle(1, L2, R2, P2)

    for p in range(2):
        def last(i, q):
            z_s[2, q] = rear(1, q)
            rear_back(1, q, cot_s[q].astype(F32))

        pairs_here(p, P2)
        unpack(p, P2, 0)
        loop(last, p)
        pack(p, DP2, 0)
        to_channels(p, (DP2,))
    for p in range(2):
        def write_out(i, q):
            out_ref[i, p * half:(p + 1) * half, :] = nt(eye_s[0:half, 0:half], z_s[2, q]).astype(BF16)

        loop(write_out, p)
    ge_s[5 * CH:6 * CH, :] = out_grad(1).astype(BF16)
    triangle_back(1, DP2, DL2, DR2)
    ge_s[4 * CH:5 * CH, :] = proj_grad(1, 4).astype(BF16)

    for p in range(2):
        def back(i, q):
            grad = front_back(1, q, cot_s[q].astype(F32))
            dz_s[0, q] = grad
            rear_back(0, q, grad.astype(F32))

        pairs_here(p, DL2)
        unpack(p, DL2, 0)
        pairs_here(p, DR2)
        unpack(p, DR2, 1)
        loop(back, p)
        pack(p, DP1, 0)
        to_channels(p, (DP1,))
    for b in range(4):
        ge_s[b * CH:(b + 1) * CH, :] = proj_grad(1, b).astype(BF16)
    ge_s[6 * CH:7 * CH, :] = proj_grad(0, 4).astype(BF16)
    ge_s[7 * CH:8 * CH, :] = out_grad(0).astype(BF16)
    scatter(ge_s, re_s, early_rows, 0)
    triangle_back(0, DP1, DL1, DR1)
    bulk(re_s, n - 1, 0).wait_recv()
    xe_s[...] = summed(re_s, n)
    across(xe_s, ye_s, 1)
    chain_s[...] = jnp.zeros_like(chain_s)
    for p in range(2):
        def end(i, q):
            grad = front_back(0, q, dz_s[0, q].astype(F32))
            dz_s[1, q] = grad
            chain_s[...] += grad.astype(F32) * sc_s[pl.ds(q, 1), :]

        def write_grad(i, q):
            pg_ref[i, p * half:(p + 1) * half, :] = nt(eye_s[0:half, 0:half], dz_s[1, q]).astype(BF16)

        pairs_here(p, DL1)
        unpack(p, DL1, 0)
        pairs_here(p, DR1)
        unpack(p, DR1, 1)
        loop(end, p)
        for b in range(4):
            if p == 0:
                acc_s[b] = proj_grad(0, b, 0)
            else:
                gf_s[b * CH:(b + 1) * CH, :] = (acc_s[b] + proj_grad(0, b, 1)).astype(BF16)
        if p == 0:
            loop(write_grad, 0)
    scatter(gf_s, rf_s, late_rows, 3)
    column = jnp.sum(chain_s[...], axis=1, keepdims=True)
    cg_s[...] = jnp.sum(diag * column, axis=0, keepdims=True)
    cr_s[me] = cg_s[...]
    spread(cg_s, cr_s, 6)
    loop(write_grad, 1)

    bulk(ye_s, dp - 1, 1).wait_recv()
    ae_s[me] = (summed(ye_s, dp) * inverse).astype(BF16)
    spread(ae_s.at[me], ae_s, 2)
    bulk(rf_s, n - 1, 3).wait_recv()
    xf_s[...] = summed(rf_s, n)
    across(xf_s, yf_s, 4)
    bulk(cr_s, n - 1, 6).wait_recv()
    cx_s[...] = summed(cr_s, n)
    across(cx_s, cy_s, 7)
    bulk(yf_s, dp - 1, 4).wait_recv()
    af_s[me] = (summed(yf_s, dp) * inverse).astype(BF16)
    spread(af_s.at[me], af_s, 5)
    bulk(cy_s, dp - 1, 7).wait_recv()
    gchain_ref[...] = summed(cy_s, dp) * inverse
    bulk(ae_s, n - 1, 2).wait_recv()
    full = ae_s[...].reshape(8 * CH, CH).astype(F32)
    for b in range(5):
        gproj_ref[1, :, b * CH:(b + 1) * CH] = full[b * CH:(b + 1) * CH]
    gout_ref[1] = full[5 * CH:6 * CH]
    gproj_ref[0, :, 4 * CH:5 * CH] = full[6 * CH:7 * CH]
    gout_ref[0] = full[7 * CH:8 * CH]

    def drain(a, carry):
        sent(a)
        return carry

    lax.fori_loop(0, 12, drain, 0)
    for r, count, k in ((re_s, n, 0), (ye_s, dp, 1), (ae_s, n, 2), (rf_s, n, 3), (yf_s, dp, 4), (cr_s, n, 6), (cy_s, dp, 7)):
        bulk(r, count - 1, k).wait_send()
    bulk(af_s, n - 1, 5).wait_recv()
    full = af_s[...].reshape(4 * CH, CH).astype(F32)
    for b in range(4):
        gproj_ref[0, :, b * CH:(b + 1) * CH] = full[b * CH:(b + 1) * CH]
    bulk(af_s, n - 1, 5).wait_send()


def hand_over(*refs):
    count = (len(refs) - 2) // 3
    given, outs, held = refs[:count], refs[count:2 * count], refs[2 * count:3 * count]
    in_sem, out_sem = refs[-2:]
    fetched = [pltpu.make_async_copy(given[k], held[k], in_sem.at[k]) for k in range(count)]
    put = [pltpu.make_async_copy(held[k], outs[k], out_sem.at[k]) for k in range(count)]
    for copy in fetched:
        copy.start()
    for k in range(count):
        fetched[k].wait()
        put[k].start()
    for copy in put:
        copy.wait()


def body(n, dp, pair_in, residue_mask, chain_index, chain_bias, proj_weight, out_weight, cotangent):
    width = n * ROWS
    group = CH // n
    early_rows, late_rows = 8 * CH // n, 4 * CH // n
    tensor = (2 * ROWS, CH, width // 2)
    line = (2 * ROWS, 1, width // 2)
    vmem = pl.BlockSpec(memory_space=pltpu.VMEM)
    shapes = [
        jax.ShapeDtypeStruct((ROWS, width, CH), BF16),
        jax.ShapeDtypeStruct((ROWS, width, CH), BF16),
        jax.ShapeDtypeStruct((2, CH, 5 * CH), F32),
        jax.ShapeDtypeStruct((2, CH, CH), F32),
        jax.ShapeDtypeStruct((1, CH), F32),
    ]
    scratch = [
        pltpu.VMEM((CH, CH), BF16),
        pltpu.VMEM((256, 256), BF16),
        pltpu.VMEM((256, 256), BF16),
        pltpu.VMEM((2, 5 * CH, CH), BF16),
        pltpu.VMEM((2, CH, CH), BF16),
        pltpu.VMEM((CH, 1), F32),
        pltpu.VMEM((2 * ROWS, width // 2), F32),
        pltpu.VMEM((2 * ROWS, width // 2), F32),
        pltpu.VMEM((3,) + tensor, BF16),
        pltpu.VMEM(tensor, BF16),
        pltpu.VMEM((2,) + tensor, BF16),
        pltpu.VMEM((2,) + tensor, BF16),
        pltpu.VMEM((2,) + tensor, F32),
        pltpu.VMEM((2,) + line, F32),
        pltpu.VMEM((2, 4) + tensor, F32),
        pltpu.VMEM((2,) + tensor, F32),
        pltpu.VMEM((2,) + tensor, F32),
        pltpu.VMEM((2,) + tensor, BF16),
        pltpu.VMEM((2,) + line, F32),
        pltpu.VMEM((2,) + tensor, F32),
        pltpu.VMEM((2,) + tensor, BF16),
        pltpu.VMEM((2, 5) + tensor, BF16),
        pltpu.VMEM((2,) + tensor, BF16),
        pltpu.VMEM((2,) + tensor, F32),
        pltpu.VMEM((2, 2, group, width, width), BF16),
        pltpu.VMEM((CH, width // 2), F32),
        pltpu.VMEM((4, CH, CH), F32),
        pltpu.VMEM((12, n, group * ROWS, width), BF16),
        pltpu.VMEM((12, n, group * ROWS, width), BF16),
        pltpu.VMEM((8 * CH, CH), BF16),
        pltpu.VMEM((n, early_rows, CH), BF16),
        pltpu.VMEM((n, early_rows, CH), BF16),
        pltpu.VMEM((4 * CH, CH), BF16),
        pltpu.VMEM((n, late_rows, CH), BF16),
        pltpu.VMEM((n, late_rows, CH), BF16),
        pltpu.VMEM((early_rows, CH), F32),
        pltpu.VMEM((dp, early_rows, CH), F32),
        pltpu.VMEM((late_rows, CH), F32),
        pltpu.VMEM((dp, late_rows, CH), F32),
        pltpu.VMEM((1, CH), F32),
        pltpu.VMEM((n, 1, CH), F32),
        pltpu.VMEM((1, CH), F32),
        pltpu.VMEM((dp, 1, CH), F32),
        pltpu.SemaphoreType.DMA((12,)),
        pltpu.SemaphoreType.DMA((12, 3)),
        pltpu.SemaphoreType.DMA((8,)),
        pltpu.SemaphoreType.DMA((8,)),
    ]
    results = pl.pallas_call(
        functools.partial(kernel, n, dp),
        out_shape=shapes,
        in_specs=[vmem] * 7,
        out_specs=[vmem] * 5,
        scratch_shapes=scratch,
        compiler_params=pltpu.CompilerParams(
            collective_id=0, has_side_effects=True, vmem_limit_bytes=62 * 1024 * 1024
        ),
    )(
        pair_in[0], residue_mask, chain_index, chain_bias.reshape(1, CH),
        proj_weight, out_weight, cotangent[0],
    )
    anywhere = pl.BlockSpec(memory_space=pl.ANY)
    out_pair, pair_grad, grad_proj, grad_out, grad_chain = pl.pallas_call(
        hand_over,
        out_shape=shapes,
        in_specs=[anywhere] * 5,
        out_specs=[anywhere] * 5,
        scratch_shapes=[pltpu.VMEM(shape.shape, shape.dtype) for shape in shapes]
        + [pltpu.SemaphoreType.DMA((5,)), pltpu.SemaphoreType.DMA((5,))],
        compiler_params=pltpu.CompilerParams(vmem_limit_bytes=62 * 1024 * 1024),
    )(*results)
    return out_pair[None], pair_grad[None], grad_proj, grad_out, grad_chain.reshape(CH)


def solution(mesh):
    n, dp = mesh.shape["dap"], mesh.shape["dp"]
    rows = P("dp", "dap", None, None)
    return jax.shard_map(
        functools.partial(body, n, dp),
        mesh=mesh,
        in_specs=(rows, P("dp", None), P("dp", None), P(), P(), P(), rows),
        out_specs=(rows, rows, P(), P(), P()),
        check_vma=False,
    )
```

time: 153 us -> 122 us (0.80)
  Pallas kernels: 146 us -> 121 us
  local copies, waits for them, and re-layouts: 5.4 us -> 0 us
    pallas_call x1, Pallas kernels: 146 us -> 119 us  [body(): pl.pallas_call(functools.partial(kernel, n, dp), out_shape=shapes, in_spe...]
    unnamed x13 -> x0, local copies, waits for them, and re-layouts: 5.4 us -> none
    pallas_call x0 -> x1, Pallas kernels: none -> 2.37 us  [body(): pl.pallas_call(hand_over, out_shape=shapes, in_specs=[anywhere] * 5, out_...]
where the time goes in v1:
time: 122 us
  Pallas kernels  121 us (99%)
    pallas_call x1, Pallas kernels, body(): pl.pallas_call(functools.partial(kernel, n, dp), out_shape=shapes, in_spe...  119 us

profile of v1, /device:TPU:1, one launch (start us, length us, event | category | flops | bytes accessed | tf_op | source)
XLA Modules:
  0.0 122.2 jit_solution(8163567549932149594)
XLA Ops:
  0.6 119.0 %shard_map.110 = (bf16[8,256,128]{2,1,0:T(8,128)(2,1)}, bf16[8,256,128]{2,1,0:T(8,128)(2,1)}, f32[2,128,640]{2,1,0:T(8,128)}, f32[2,128,128]{2,1,0:T(8,128)}, f32[1,128]{1,0:T(1,128)}) custom-call(bf16[8,256,128]{2,1,0:T(8,128)(2,1)} %bitcast.6, s32[1,256]{1,0:T(1,128)} %mask_ref.1, s32[1,256]{1,0:T(1,128)} %chain_ref.1, f32[1,128]{1,0:T(1,128)} %bitcast.8, ...), custom_call_target="tpu_custom_call" | custom-call | tf_op jit(solution)/shard_map/pallas_call | solution.py:566
  119.7 2.4 %shard_map.111 = (bf16[8,256,128]{2,1,0:T(8,128)(2,1)}, bf16[8,256,128]{2,1,0:T(8,128)(2,1)}, f32[2,128,640]{2,1,0:T(8,128)}, f32[2,128,128]{2,1,0:T(8,128)}, f32[1,128]{1,0:T(1,128)}) custom-call(bf16[8,256,128]{2,1,0:T(8,128)(2,1)} %get-tuple-element.15.refs_0_, bf16[8,256,128]{2,1,0:T(8,128)(2,1)} %get-tuple-element.16.refs_1_, ...), custom_call_target="tpu_custom_call" | custom-call | tf_op jit(solution)/shard_map/pallas_call | solution.py:580

commit v2 on v1

--- a/solution.py
+++ b/solution.py
@@ -58,8 +58,8 @@
     eye_s, pf_s, pt_s, pwt_s, owt_s, bias_s, pm_s, sc_s,
     z_s, cot_s, dz_s, nb_s, nrm_s, istd_s, side_s, gate_s, pn_s, pnb_s, pstd_s, upd_s,
     dupd_s, dproj_s, edge_s, in_s, mats_s, chain_s, acc_s,
-    send, recv, ge_s, re_s, ae_s, gf_s, rf_s, af_s, xe_s, ye_s, xf_s, yf_s, cg_s, cr_s, cx_s, cy_s,
-    send_sem, recv_sem, gsend_sem, grecv_sem,
+    send, recv, ge_s, re_s, ae_s, gf_s, rf_s, af_s, xe_s, ye_s, xf_s, yf_s, cg_s, cr_s, cx_s, cy_s, outv_s, pgv_s,
+    send_sem, recv_sem, gsend_sem, grecv_sem, put_sem,
 ):
     width = n * ROWS
     half = width // 2
@@ -87,14 +87,14 @@
 
     eye_s[...] = one_hot(CH, CH, lambda r, q: r == q).astype(BF16)
     pf_s[...] = one_hot(256, 256, lambda r, q: q == (r % ROWS) * BLOCK + r // ROWS).astype(BF16)
-    pt_s[...] = one_hot(256, 256, lambda r, q: q == (r % BLOCK) * ROWS + r // BLOCK).astype(BF16)
     diag = one_hot(CH, CH, lambda r, q: r == q)
     bias_s[...] = jnp.sum(diag * bias_ref[...], axis=1, keepdims=True)
-    eye = eye_s[...]
-    for t in range(2):
-        for b in range(5):
-            pwt_s[t, b * CH:(b + 1) * CH, :] = nt(eye, pw_ref[t, :, b * CH:(b + 1) * CH]).astype(BF16)
-        owt_s[t] = nt(eye, ow_ref[t]).astype(BF16)
+
+    def turn_weight(t, b):
+        pwt_s[t, b * CH:(b + 1) * CH, :] = nt(eye_s[...], pw_ref[t, :, b * CH:(b + 1) * CH]).astype(BF16)
+
+    for b in range(4):
+        turn_weight(0, b)
     live = mask_ref[...].astype(F32)
     chain = chain_ref[...].astype(F32)
     own = one_hot(ROWS, width, lambda r, q: q == r + ROWS * me)
@@ -104,18 +104,32 @@
         pm_s[p * ROWS:(p + 1) * ROWS, :] = pair_mask[:, p * half:(p + 1) * half]
         sc_s[p * ROWS:(p + 1) * ROWS, :] = same[:, p * half:(p + 1) * half]
 
-    def partner_of(t):
-        y, z, x = me // 8, (me // 4) % 2, me % 4
-        ny, nz, nx = (y + t // 8) % 4, (z + (t // 4) % 2) % 2, (x + t % 4) % 4
-        return (ny * 2 + nz) * 4 + nx if n == 32 else (me + t) % n
+    if n == 32:
+        row, plane, column = me // 8, (me // 4) % 2, me % 4
+        planes = [4 * lax.rem(plane + k, 2) for k in range(2)]
+        columns = [lax.rem(column + k, 4) for k in range(4)]
+
+    def to_all(start):
+        if n != 32:
+            lax.fori_loop(1, n, lambda t, carry: (start(lax.rem(me + t, n)), carry)[1], 0)
+            return
+
+        def some(turn, first):
+            lines = [8 * lax.rem(row + turn + k, 4) for k in range(4)]
+            for k in (1, 2, 3, 0):
+                for h in (1, 0):
+                    if not (first and k == 0 and h == 0):
+                        start(lines[k] + planes[h] + columns[k])
+
+        some(0, True)
+        lax.fori_loop(1, 4, lambda turn, carry: (some(turn, False), carry)[1], 0)
 
     def push(messages):
         for a, r0, rn, p, k in messages:
             at = (a, pl.ds(me, 1), slice(r0, r0 + rn), slice(p * half, (p + 1) * half))
             recv[at] = send[at]
 
-        def go(t, carry):
-            to = partner_of((t * 11) % n)
+        def go(to):
             for a, r0, rn, p, k in messages:
                 part = (pl.ds(r0, rn), pl.ds(p * half, half))
                 pltpu.make_async_remote_copy(
@@ -123,9 +137,8 @@
                     send_sem=send_sem.at[a], recv_sem=recv_sem.at[a, k],
                     device_id={"dap": to}, device_id_type=MESH,
                 ).start()
-            return carry
-
-        lax.fori_loop(1, n, go, 0)
+
+        to_all(go)
 
     def arrived(a, r0, rn, p, k):
         part = (a, pl.ds(0, n - 1), pl.ds(r0, rn), pl.ds(p * half, half))
@@ -225,14 +238,15 @@
         normed, inv = norm(z.astype(F32))
         nb = normed.astype(BF16)
         nrm_s[t, q], istd_s[t, q], nb_s[t, q] = normed, inv, nb
-        pm = pm_s[pl.ds(q, 1), :]
-        for e in range(2):
-            value = nn(pwt_s[t, 2 * e * CH:(2 * e + 1) * CH, :], nb)
-            scale = pm * sigmoid(nn(pwt_s[t, (2 * e + 1) * CH:(2 * e + 2) * CH, :], nb))
-            edge = scale * value
-            side_s[t, 2 * e, q] = scale
-            side_s[t, 2 * e + 1, q] = edge
-            edge_s[e, q] = edge.astype(BF16)
+        make_edge(t, 0, q, nb)
+
+    def make_edge(t, e, q, nb):
+        value = nn(pwt_s[t, 2 * e * CH:(2 * e + 1) * CH, :], nb)
+        scale = pm_s[pl.ds(q, 1), :] * sigmoid(nn(pwt_s[t, (2 * e + 1) * CH:(2 * e + 2) * CH, :], nb))
+        edge = scale * value
+        side_s[t, 2 * e, q] = scale
+        side_s[t, 2 * e + 1, q] = edge
+        edge_s[e, q] = edge.astype(BF16)
 
     def gates(t):
         def step(q, carry):
@@ -256,15 +270,16 @@
         g = nn(ow_ref[t], dupd)
         edge_s[0, q] = norm_back(pn_s[t, q], pstd_s[t, q], g).astype(BF16)
 
-    def front_back(t, q, up):
-        h = nn(pw_ref[t, :, 4 * CH:5 * CH], dproj_s[t, 4, q])
+    def edge_back(t, q):
         for e in range(2):
             grad, scale = in_s[e, q], side_s[t, 2 * e, q]
-            first = (grad * scale).astype(BF16)
-            second = (grad * side_s[t, 2 * e + 1, q] * (1.0 - scale)).astype(BF16)
-            dproj_s[t, 2 * e, q], dproj_s[t, 2 * e + 1, q] = first, second
-            h += nn(pw_ref[t, :, 2 * e * CH:(2 * e + 1) * CH], first)
-            h += nn(pw_ref[t, :, (2 * e + 1) * CH:(2 * e + 2) * CH], second)
+            dproj_s[t, 2 * e, q] = (grad * scale).astype(BF16)
+            dproj_s[t, 2 * e + 1, q] = (grad * side_s[t, 2 * e + 1, q] * (1.0 - scale)).astype(BF16)
+
+    def front_back(t, q, up):
+        h = nn(pw_ref[t, :, 0:CH], dproj_s[t, 0, q])
+        for b in range(1, 5):
+            h += nn(pw_ref[t, :, b * CH:(b + 1) * CH], dproj_s[t, b, q])
         return (up + norm_back(nrm_s[t, q], istd_s[t, q], h)).astype(BF16)
 
     early_rows, late_rows = 8 * CH // n, 4 * CH // n
@@ -286,41 +301,33 @@
         return pl.ds(pl.multiple_of(at * size, size), size)
 
     def scatter(g, r, size, k):
-        r[pl.ds(me, 1)] = g[piece(me, size), :].reshape(1, size, CH)
-
-        def go(t, carry):
-            to = partner_of((t * 11) % n)
+        r[me] = g[piece(me, size), :]
+
+        def go(to):
             pltpu.make_async_remote_copy(
                 src_ref=g.at[piece(to, size)], dst_ref=r.at[me],
                 send_sem=gsend_sem.at[k], recv_sem=grecv_sem.at[k],
                 device_id={"dap": to}, device_id_type=MESH,
             ).start()
-            return carry
-
-        lax.fori_loop(1, n, go, 0)
+
+        to_all(go)
 
     def spread(x, r, k):
-        def go(t, carry):
-            to = partner_of((t * 11) % n)
+        def go(to):
             pltpu.make_async_remote_copy(
                 src_ref=x, dst_ref=r.at[me], send_sem=gsend_sem.at[k], recv_sem=grecv_sem.at[k],
                 device_id={"dap": to}, device_id_type=MESH,
             ).start()
-            return carry
-
-        lax.fori_loop(1, n, go, 0)
+
+        to_all(go)
 
     def across(x, y, k):
         y[mine] = x[...]
-
-        def go(t, carry):
+        for t in range(1, dp):
             pltpu.make_async_remote_copy(
                 src_ref=x, dst_ref=y.at[mine], send_sem=gsend_sem.at[k], recv_sem=grecv_sem.at[k],
                 device_id={"dp": lax.rem(mine + t, dp)}, device_id_type=MESH,
             ).start()
-            return carry
-
-        lax.fori_loop(1, dp, go, 0)
 
     def bulk(r, count, k):
         return pltpu.make_async_remote_copy(
@@ -351,12 +358,23 @@
             z_s[0, q] = z
             front(0, q, z)
 
+        def begin_right(i, q):
+            make_edge(0, 1, q, nb_s[0, q])
+
         loop(begin, p)
         pack(p, L1, 0)
-        pack(p, R1, 1)
         if p == 0:
             pl.semaphore_wait(barrier, n - 1 + dp - 1)
-        to_channels(p, (L1, R1))
+            to_channels(0, (L1,))
+        loop(begin_right, p)
+        pack(p, R1, 1)
+        to_channels(p, (R1,) if p == 0 else (L1, R1))
+    turn_weight(0, 4)
+    for b in range(5):
+        turn_weight(1, b)
+    for t in range(2):
+        owt_s[t] = nt(eye_s[...], ow_ref[t]).astype(BF16)
+    pt_s[...] = one_hot(256, 256, lambda r, q: q == (r % BLOCK) * ROWS + r // BLOCK).astype(BF16)
     gates(0)
     for p in range(2):
         def turn(i, q):
@@ -372,10 +390,16 @@
 
         pairs_here(p, P1)
         unpack(p, P1, 0)
+        def middle_right(i, q):
+            make_edge(1, 1, q, nb_s[1, q])
+
         loop(middle, p)
         pack(p, L2, 0)
+        if p == 0:
+            to_channels(0, (L2,))
+        loop(middle_right, p)
         pack(p, R2, 1)
-        to_channels(p, (L2, R2))
+        to_channels(p, (R2,) if p == 0 else (L2, R2))
     gates(1)
     triangle(1, L2, R2, P2)
 
@@ -391,15 +415,18 @@
         to_channels(p, (DP2,))
     for p in range(2):
         def write_out(i, q):
-            out_ref[i, p * half:(p + 1) * half, :] = nt(eye_s[0:half, 0:half], z_s[2, q]).astype(BF16)
+            outv_s[i, p * half:(p + 1) * half, :] = nt(eye_s[0:half, 0:half], z_s[2, q]).astype(BF16)
 
         loop(write_out, p)
+    put_out = pltpu.make_async_copy(outv_s, out_ref, put_sem.at[0])
+    put_out.start()
     ge_s[5 * CH:6 * CH, :] = out_grad(1).astype(BF16)
     triangle_back(1, DP2, DL2, DR2)
     ge_s[4 * CH:5 * CH, :] = proj_grad(1, 4).astype(BF16)
 
     for p in range(2):
         def back(i, q):
+            edge_back(1, q)
             grad = front_back(1, q, cot_s[q].astype(F32))
             dz_s[0, q] = grad
             rear_back(0, q, grad.astype(F32))
@@ -423,12 +450,7 @@
     chain_s[...] = jnp.zeros_like(chain_s)
     for p in range(2):
         def end(i, q):
-            grad = front_back(0, q, dz_s[0, q].astype(F32))
-            dz_s[1, q] = grad
-            chain_s[...] += grad.astype(F32) * sc_s[pl.ds(q, 1), :]
-
-        def write_grad(i, q):
-            pg_ref[i, p * half:(p + 1) * half, :] = nt(eye_s[0:half, 0:half], dz_s[1, q]).astype(BF16)
+            edge_back(0, q)
 
         pairs_here(p, DL1)
         unpack(p, DL1, 0)
@@ -441,28 +463,37 @@
             else:
                 gf_s[b * CH:(b + 1) * CH, :] = (acc_s[b] + proj_grad(0, b, 1)).astype(BF16)
         if p == 0:
-            loop(write_grad, 0)
+            bulk(ye_s, dp - 1, 1).wait_recv()
+            ae_s[me] = (summed(ye_s, dp) * inverse).astype(BF16)
+            spread(ae_s.at[me], ae_s, 2)
     scatter(gf_s, rf_s, late_rows, 3)
-    column = jnp.sum(chain_s[...], axis=1, keepdims=True)
-    cg_s[...] = jnp.sum(diag * column, axis=0, keepdims=True)
+    for p in range(2):
+        def finish(i, q):
+            grad = front_back(0, q, dz_s[0, q].astype(F32))
+            dz_s[1, q] = grad
+            chain_s[...] += grad.astype(F32) * sc_s[pl.ds(q, 1), :]
+
+        loop(finish, p)
+    column_sum = jnp.sum(chain_s[...], axis=1, keepdims=True)
+    cg_s[...] = jnp.sum(diag * column_sum, axis=0, keepdims=True)
     cr_s[me] = cg_s[...]
     spread(cg_s, cr_s, 6)
-    loop(write_grad, 1)
-
-    bulk(ye_s, dp - 1, 1).wait_recv()
-    ae_s[me] = (summed(ye_s, dp) * inverse).astype(BF16)
-    spread(ae_s.at[me], ae_s, 2)
     bulk(rf_s, n - 1, 3).wait_recv()
     xf_s[...] = summed(rf_s, n)
     across(xf_s, yf_s, 4)
+    for p in range(2):
+        def write_grad(i, q):
+            pgv_s[i, p * half:(p + 1) * half, :] = nt(eye_s[0:half, 0:half], dz_s[1, q]).astype(BF16)
+
+        loop(write_grad, p)
+    put_grad = pltpu.make_async_copy(pgv_s, pg_ref, put_sem.at[1])
+    put_grad.start()
     bulk(cr_s, n - 1, 6).wait_recv()
     cx_s[...] = summed(cr_s, n)
     across(cx_s, cy_s, 7)
     bulk(yf_s, dp - 1, 4).wait_recv()
     af_s[me] = (summed(yf_s, dp) * inverse).astype(BF16)
     spread(af_s.at[me], af_s, 5)
-    bulk(cy_s, dp - 1, 7).wait_recv()
-    gchain_ref[...] = summed(cy_s, dp) * inverse
     bulk(ae_s, n - 1, 2).wait_recv()
     full = ae_s[...].reshape(8 * CH, CH).astype(F32)
     for b in range(5):
@@ -470,6 +501,8 @@
     gout_ref[1] = full[5 * CH:6 * CH]
     gproj_ref[0, :, 4 * CH:5 * CH] = full[6 * CH:7 * CH]
     gout_ref[0] = full[7 * CH:8 * CH]
+    bulk(cy_s, dp - 1, 7).wait_recv()
+    gchain_ref[...] = summed(cy_s, dp) * inverse
 
     def drain(a, carry):
         sent(a)
@@ -478,6 +511,8 @@
     lax.fori_loop(0, 12, drain, 0)
     for r, count, k in ((re_s, n, 0), (ye_s, dp, 1), (ae_s, n, 2), (rf_s, n, 3), (yf_s, dp, 4), (cr_s, n, 6), (cy_s, dp, 7)):
         bulk(r, count - 1, k).wait_send()
+    put_out.wait()
+    put_grad.wait()
     bulk(af_s, n - 1, 5).wait_recv()
     full = af_s[...].reshape(4 * CH, CH).astype(F32)
     for b in range(4):
@@ -558,16 +593,19 @@
         pltpu.VMEM((n, 1, CH), F32),
         pltpu.VMEM((1, CH), F32),
         pltpu.VMEM((dp, 1, CH), F32),
+        pltpu.VMEM((ROWS, width, CH), BF16),
+        pltpu.VMEM((ROWS, width, CH), BF16),
         pltpu.SemaphoreType.DMA((12,)),
         pltpu.SemaphoreType.DMA((12, 3)),
         pltpu.SemaphoreType.DMA((8,)),
         pltpu.SemaphoreType.DMA((8,)),
+        pltpu.SemaphoreType.DMA((2,)),
     ]
     results = pl.pallas_call(
         functools.partial(kernel, n, dp),
         out_shape=shapes,
         in_specs=[vmem] * 7,
-        out_specs=[vmem] * 5,
+        out_specs=[pl.BlockSpec(memory_space=pl.ANY)] * 2 + [vmem] * 3,
         scratch_shapes=scratch,
         compiler_params=pltpu.CompilerParams(
             collective_id=0, has_side_effects=True, vmem_limit_bytes=62 * 1024 * 1024

time: 122 us -> 117 us (0.959)
  Pallas kernels: 121 us -> 116 us
    pallas_call x1, Pallas kernels: 119 us -> 114 us  [body(): pl.pallas_call(functools.partial(kernel, n, dp), out_shape=shapes, in_spe...]
where the time goes in v2:
time: 117 us
  Pallas kernels  116 us (99%)
    pallas_call x1, Pallas kernels, body(): pl.pallas_call(functools.partial(kernel, n, dp), out_shape=shapes, in_spe...  114 us
    pallas_call x1, Pallas kernels, body(): pl.pallas_call(hand_over, out_shape=shapes, in_specs=[anywhere] * 5, out_...  2.37 us

profile of v2, /device:TPU:1, one launch (start us, length us, event | category | flops | bytes accessed | tf_op | source)
XLA Modules:
  0.0 116.9 jit_solution(16829388846758395570)
XLA Ops:
  0.6 113.7 %shard_map.110 = (bf16[8,256,128]{2,1,0:T(8,128)(2,1)}, bf16[8,256,128]{2,1,0:T(8,128)(2,1)}, f32[2,128,640]{2,1,0:T(8,128)}, f32[2,128,128]{2,1,0:T(8,128)}, f32[1,128]{1,0:T(1,128)}) custom-call(bf16[8,256,128]{2,1,0:T(8,128)(2,1)} %bitcast.6, s32[1,256]{1,0:T(1,128)} %mask_ref.1, s32[1,256]{1,0:T(1,128)} %chain_ref.1, f32[1,128]{1,0:T(1,128)} %bitcast.8, ...), custom_call_target="tpu_custom_call" | custom-call | tf_op jit(solution)/shard_map/pallas_call | solution.py:604
  114.4 2.4 %shard_map.111 = (bf16[8,256,128]{2,1,0:T(8,128)(2,1)}, bf16[8,256,128]{2,1,0:T(8,128)(2,1)}, f32[2,128,640]{2,1,0:T(8,128)}, f32[2,128,128]{2,1,0:T(8,128)}, f32[1,128]{1,0:T(1,128)}) custom-call(bf16[8,256,128]{2,1,0:T(8,128)(2,1)} %get-tuple-element.15.refs_0_, bf16[8,256,128]{2,1,0:T(8,128)(2,1)} %get-tuple-element.16.refs_1_, ...), custom_call_target="tpu_custom_call" | custom-call | tf_op jit(solution)/shard_map/pallas_call | solution.py:618

commit v3 on v2

--- a/solution.py
+++ b/solution.py
@@ -114,15 +114,12 @@
             lax.fori_loop(1, n, lambda t, carry: (start(lax.rem(me + t, n)), carry)[1], 0)
             return
 
-        def some(turn, first):
-            lines = [8 * lax.rem(row + turn + k, 4) for k in range(4)]
-            for k in (1, 2, 3, 0):
-                for h in (1, 0):
-                    if not (first and k == 0 and h == 0):
-                        start(lines[k] + planes[h] + columns[k])
-
-        some(0, True)
-        lax.fori_loop(1, 4, lambda turn, carry: (some(turn, False), carry)[1], 0)
+        lines = [8 * lax.rem(row + k, 4) for k in range(4)]
+        away = (0, 1, 2, 1)
+        order = [(k, h, c) for k in range(4) for h in range(2) for c in range(4)]
+        order.sort(key=lambda d: (-(away[d[0]] + d[1] + away[d[2]]), (d[0] + 2 * d[2] + d[1]) % 4))
+        for k, h, c in order[:-1]:
+            start(lines[k] + planes[h] + columns[c])
 
     def push(messages):
         for a, r0, rn, p, k in messages:
@@ -172,7 +169,8 @@
     def to_pairs(cc, items):
         push([(a, cc * half_rows, half_rows, 0, 0) for a in items])
         if cc == 1:
-            push([(a, 0, rows, 1, 1) for a in items])
+            for a in items:
+                push([(a, 0, rows, 1, 1)])
 
     def pairs_here(p, a):
         arrived(a, 0, rows, p, p)
@@ -241,9 +239,9 @@
         make_edge(t, 0, q, nb)
 
     def make_edge(t, e, q, nb):
-        value = nn(pwt_s[t, 2 * e * CH:(2 * e + 1) * CH, :], nb)
-        scale = pm_s[pl.ds(q, 1), :] * sigmoid(nn(pwt_s[t, (2 * e + 1) * CH:(2 * e + 2) * CH, :], nb))
-        edge = scale * value
+        both = nn(pwt_s[t, 2 * e * CH:(2 * e + 2) * CH, :], nb)
+        scale = pm_s[pl.ds(q, 1), :] * sigmoid(both[CH:])
+        edge = scale * both[:CH]
         side_s[t, 2 * e, q] = scale
         side_s[t, 2 * e + 1, q] = edge
         edge_s[e, q] = edge.astype(BF16)
@@ -266,20 +264,22 @@
         gate = gate_s[t, q]
         dupd = (up * gate).astype(BF16)
         dupd_s[t, q] = dupd
-        dproj_s[t, 4, q] = (up * upd_s[t, q] * gate * (1.0 - gate)).astype(BF16)
         g = nn(ow_ref[t], dupd)
         edge_s[0, q] = norm_back(pn_s[t, q], pstd_s[t, q], g).astype(BF16)
 
-    def edge_back(t, q):
-        for e in range(2):
-            grad, scale = in_s[e, q], side_s[t, 2 * e, q]
-            dproj_s[t, 2 * e, q] = (grad * scale).astype(BF16)
-            dproj_s[t, 2 * e + 1, q] = (grad * side_s[t, 2 * e + 1, q] * (1.0 - scale)).astype(BF16)
+    def gate_back(t, q, up):
+        gate = gate_s[t, q]
+        dproj_s[t, q, 4 * CH:5 * CH, :] = (up * upd_s[t, q] * gate * (1.0 - gate)).astype(BF16)
+
+    def edge_back(t, e, q):
+        grad, scale = in_s[e, q], side_s[t, 2 * e, q]
+        dproj_s[t, q, 2 * e * CH:(2 * e + 1) * CH, :] = (grad * scale).astype(BF16)
+        dproj_s[t, q, (2 * e + 1) * CH:(2 * e + 2) * CH, :] = (
+            grad * side_s[t, 2 * e + 1, q] * (1.0 - scale)
+        ).astype(BF16)
 
     def front_back(t, q, up):
-        h = nn(pw_ref[t, :, 0:CH], dproj_s[t, 0, q])
-        for b in range(1, 5):
-            h += nn(pw_ref[t, :, b * CH:(b + 1) * CH], dproj_s[t, b, q])
+        h = nn(pw_ref[t], dproj_s[t, q])
         return (up + norm_back(nrm_s[t, q], istd_s[t, q], h)).astype(BF16)
 
     early_rows, late_rows = 8 * CH // n, 4 * CH // n
@@ -292,9 +292,9 @@
 
     def proj_grad(t, b, p=None):
         first, last = (0, 2 * ROWS) if p is None else (p * ROWS, (p + 1) * ROWS)
-        total = nt(nb_s[t, first], dproj_s[t, b, first])
+        total = nt(nb_s[t, first], dproj_s[t, first, b * CH:(b + 1) * CH, :])
         for q in range(first + 1, last):
-            total += nt(nb_s[t, q], dproj_s[t, b, q])
+            total += nt(nb_s[t, q], dproj_s[t, q, b * CH:(b + 1) * CH, :])
         return total
 
     def piece(at, size):
@@ -417,7 +417,11 @@
         def write_out(i, q):
             outv_s[i, p * half:(p + 1) * half, :] = nt(eye_s[0:half, 0:half], z_s[2, q]).astype(BF16)
 
+        def gate_two(i, q):
+            gate_back(1, q, cot_s[q].astype(F32))
+
         loop(write_out, p)
+        loop(gate_two, p)
     put_out = pltpu.make_async_copy(outv_s, out_ref, put_sem.at[0])
     put_out.start()
     ge_s[5 * CH:6 * CH, :] = out_grad(1).astype(BF16)
@@ -426,13 +430,17 @@
 
     for p in range(2):
         def back(i, q):
-            edge_back(1, q)
+            edge_back(1, 1, q)
             grad = front_back(1, q, cot_s[q].astype(F32))
             dz_s[0, q] = grad
             rear_back(0, q, grad.astype(F32))
 
+        def back_left(i, q):
+            edge_back(1, 0, q)
+
         pairs_here(p, DL2)
         unpack(p, DL2, 0)
+        loop(back_left, p)
         pairs_here(p, DR2)
         unpack(p, DR2, 1)
         loop(back, p)
@@ -440,6 +448,11 @@
         to_channels(p, (DP1,))
     for b in range(4):
         ge_s[b * CH:(b + 1) * CH, :] = proj_grad(1, b).astype(BF16)
+    for p in range(2):
+        def gate_one(i, q):
+            gate_back(0, q, dz_s[0, q].astype(F32))
+
+        loop(gate_one, p)
     ge_s[6 * CH:7 * CH, :] = proj_grad(0, 4).astype(BF16)
     ge_s[7 * CH:8 * CH, :] = out_grad(0).astype(BF16)
     scatter(ge_s, re_s, early_rows, 0)
@@ -449,19 +462,18 @@
     across(xe_s, ye_s, 1)
     chain_s[...] = jnp.zeros_like(chain_s)
     for p in range(2):
-        def end(i, q):
-            edge_back(0, q)
-
-        pairs_here(p, DL1)
-        unpack(p, DL1, 0)
-        pairs_here(p, DR1)
-        unpack(p, DR1, 1)
-        loop(end, p)
-        for b in range(4):
-            if p == 0:
-                acc_s[b] = proj_grad(0, b, 0)
-            else:
-                gf_s[b * CH:(b + 1) * CH, :] = (acc_s[b] + proj_grad(0, b, 1)).astype(BF16)
+        for e in range(2):
+            def end(i, q):
+                edge_back(0, e, q)
+
+            pairs_here(p, (DL1, DR1)[e])
+            unpack(p, (DL1, DR1)[e], e)
+            loop(end, p)
+            for b in (2 * e, 2 * e + 1):
+                if p == 0:
+                    acc_s[b] = proj_grad(0, b, 0)
+                else:
+                    gf_s[b * CH:(b + 1) * CH, :] = (acc_s[b] + proj_grad(0, b, 1)).astype(BF16)
         if p == 0:
             bulk(ye_s, dp - 1, 1).wait_recv()
             ae_s[me] = (summed(ye_s, dp) * inverse).astype(BF16)
@@ -571,7 +583,7 @@
         pltpu.VMEM((2,) + line, F32),
         pltpu.VMEM((2,) + tensor, F32),
         pltpu.VMEM((2,) + tensor, BF16),
-        pltpu.VMEM((2, 5) + tensor, BF16),
+        pltpu.VMEM((2, 2 * ROWS, 5 * CH, width // 2), BF16),
         pltpu.VMEM((2,) + tensor, BF16),
         pltpu.VMEM((2,) + tensor, F32),
         pltpu.VMEM((2, 2, group, width, width), BF16),

time: 117 us -> 112 us (0.957)
  Pallas kernels: 116 us -> 111 us
    pallas_call x1, Pallas kernels: 114 us -> 109 us  [body(): pl.pallas_call(functools.partial(kernel, n, dp), out_shape=shapes, in_spe...]
where the time goes in v3:
time: 112 us
  Pallas kernels  111 us (99%)
    pallas_call x1, Pallas kernels, body(): pl.pallas_call(functools.partial(kernel, n, dp), out_shape=shapes, in_spe...  109 us
    pallas_call x1, Pallas kernels, body(): pl.pallas_call(hand_over, out_shape=shapes, in_specs=[anywhere] * 5, out_...  2.37 us

profile of v3, /device:TPU:1, one launch (start us, length us, event | category | flops | bytes accessed | tf_op | source)
XLA Modules:
  0.0 111.8 jit_solution(11652337497252947174)
XLA Ops:
  0.6 108.7 %shard_map.110 = (bf16[8,256,128]{2,1,0:T(8,128)(2,1)}, bf16[8,256,128]{2,1,0:T(8,128)(2,1)}, f32[2,128,640]{2,1,0:T(8,128)}, f32[2,128,128]{2,1,0:T(8,128)}, f32[1,128]{1,0:T(1,128)}) custom-call(bf16[8,256,128]{2,1,0:T(8,128)(2,1)} %bitcast.6, s32[1,256]{1,0:T(1,128)} %mask_ref.1, s32[1,256]{1,0:T(1,128)} %chain_ref.1, f32[1,128]{1,0:T(1,128)} %bitcast.8, ...), custom_call_target="tpu_custom_call" | custom-call | tf_op jit(solution)/shard_map/pallas_call | solution.py:616
  109.3 2.4 %shard_map.111 = (bf16[8,256,128]{2,1,0:T(8,128)(2,1)}, bf16[8,256,128]{2,1,0:T(8,128)(2,1)}, f32[2,128,640]{2,1,0:T(8,128)}, f32[2,128,128]{2,1,0:T(8,128)}, f32[1,128]{1,0:T(1,128)}) custom-call(bf16[8,256,128]{2,1,0:T(8,128)(2,1)} %get-tuple-element.15.refs_0_, bf16[8,256,128]{2,1,0:T(8,128)(2,1)} %get-tuple-element.16.refs_1_, ...), custom_call_target="tpu_custom_call" | custom-call | tf_op jit(solution)/shard_map/pallas_call | solution.py:630

commit v4 on v3

--- a/solution.py
+++ b/solution.py
@@ -53,8 +53,9 @@
 
 
 def kernel(
-    n, dp, pair_ref, mask_ref, chain_ref, bias_ref, pw_ref, ow_ref, cot_ref,
+    n, dp, pair_in, mask_in, chain_in, bias_in, pw_in, ow_in, cot_in,
     out_ref, pg_ref, gproj_ref, gout_ref, gchain_ref,
+    pair_ref, mask_ref, chain_ref, bias_ref, pw_ref, ow_ref, cot_ref, load_sem,
     eye_s, pf_s, pt_s, pwt_s, owt_s, bias_s, pm_s, sc_s,
     z_s, cot_s, dz_s, nb_s, nrm_s, istd_s, side_s, gate_s, pn_s, pnb_s, pstd_s, upd_s,
     dupd_s, dproj_s, edge_s, in_s, mats_s, chain_s, acc_s,
@@ -71,6 +72,13 @@
     me = lax.axis_index("dap")
     mine = lax.axis_index("dp")
 
+    pairs = (
+        (bias_in, bias_ref), (mask_in, mask_ref), (chain_in, chain_ref), (pw_in, pw_ref),
+        (pair_in, pair_ref), (ow_in, ow_ref), (cot_in, cot_ref),
+    )
+    loads = [pltpu.make_async_copy(given, held, load_sem.at[k]) for k, (given, held) in enumerate(pairs)]
+    for load in loads:
+        load.start()
     barrier = pltpu.get_barrier_semaphore()
 
     def greet(t, carry):
@@ -88,6 +96,8 @@
     eye_s[...] = one_hot(CH, CH, lambda r, q: r == q).astype(BF16)
     pf_s[...] = one_hot(256, 256, lambda r, q: q == (r % ROWS) * BLOCK + r // ROWS).astype(BF16)
     diag = one_hot(CH, CH, lambda r, q: r == q)
+    for load in loads[:4]:
+        load.wait()
     bias_s[...] = jnp.sum(diag * bias_ref[...], axis=1, keepdims=True)
 
     def turn_weight(t, b):
@@ -351,6 +361,7 @@
 
         lax.fori_loop(0, ROWS, step, 0, unroll=8)
 
+    loads[4].wait()
     for p in range(2):
         def begin(i, q):
             x = nt(eye_s[...], pair_ref[i, p * half:(p + 1) * half, :])
@@ -369,6 +380,8 @@
         loop(begin_right, p)
         pack(p, R1, 1)
         to_channels(p, (R1,) if p == 0 else (L1, R1))
+    loads[5].wait()
+    loads[6].wait()
     turn_weight(0, 4)
     for b in range(5):
         turn_weight(1, b)
@@ -536,13 +549,22 @@
     count = (len(refs) - 2) // 3
     given, outs, held = refs[:count], refs[count:2 * count], refs[2 * count:3 * count]
     in_sem, out_sem = refs[-2:]
-    fetched = [pltpu.make_async_copy(given[k], held[k], in_sem.at[k]) for k in range(count)]
-    put = [pltpu.make_async_copy(held[k], outs[k], out_sem.at[k]) for k in range(count)]
+    parts = []
+    for k in range(count):
+        lead = given[k].shape[0]
+        step = max(1, lead // 4)
+        parts += [(k, pl.ds(at, step)) for at in range(0, lead, step)]
+    fetched = [
+        pltpu.make_async_copy(given[k].at[at], held[k].at[at], in_sem.at[m]) for m, (k, at) in enumerate(parts)
+    ]
+    put = [
+        pltpu.make_async_copy(held[k].at[at], outs[k].at[at], out_sem.at[m]) for m, (k, at) in enumerate(parts)
+    ]
     for copy in fetched:
         copy.start()
-    for k in range(count):
-        fetched[k].wait()
-        put[k].start()
+    for m in range(len(parts)):
+        fetched[m].wait()
+        put[m].start()
     for copy in put:
         copy.wait()
 
@@ -562,6 +584,14 @@
         jax.ShapeDtypeStruct((1, CH), F32),
     ]
     scratch = [
+        pltpu.VMEM((ROWS, width, CH), BF16),
+        pltpu.VMEM((1, width), jnp.int32),
+        pltpu.VMEM((1, width), jnp.int32),
+        pltpu.VMEM((1, CH), F32),
+        pltpu.VMEM((2, CH, 5 * CH), BF16),
+        pltpu.VMEM((2, CH, CH), BF16),
+        pltpu.VMEM((ROWS, width, CH), BF16),
+        pltpu.SemaphoreType.DMA((7,)),
         pltpu.VMEM((CH, CH), BF16),
         pltpu.VMEM((256, 256), BF16),
         pltpu.VMEM((256, 256), BF16),
@@ -616,7 +646,7 @@
     results = pl.pallas_call(
         functools.partial(kernel, n, dp),
         out_shape=shapes,
-        in_specs=[vmem] * 7,
+        in_specs=[pl.BlockSpec(memory_space=pl.ANY)] * 7,
         out_specs=[pl.BlockSpec(memory_space=pl.ANY)] * 2 + [vmem] * 3,
         scratch_shapes=scratch,
         compiler_params=pltpu.CompilerParams(
@@ -633,7 +663,7 @@
         in_specs=[anywhere] * 5,
         out_specs=[anywhere] * 5,
         scratch_shapes=[pltpu.VMEM(shape.shape, shape.dtype) for shape in shapes]
-        + [pltpu.SemaphoreType.DMA((5,)), pltpu.SemaphoreType.DMA((5,))],
+        + [pltpu.SemaphoreType.DMA((13,)), pltpu.SemaphoreType.DMA((13,))],
         compiler_params=pltpu.CompilerParams(vmem_limit_bytes=62 * 1024 * 1024),
     )(*results)
     return out_pair[None], pair_grad[None], grad_proj, grad_out, grad_chain.reshape(CH)

time: 112 us -> 111 us (level)
  no operation moved by 1% of the time
where the time goes in v4:
time: 111 us
  Pallas kernels  110 us (99%)
    pallas_call x1, Pallas kernels, body(): pl.pallas_call(functools.partial(kernel, n, dp), out_shape=shapes, in_spe...  108 us
    pallas_call x1, Pallas kernels, body(): pl.pallas_call(hand_over, out_shape=shapes, in_specs=[anywhere] * 5, out_...  2.49 us

profile of v4, /device:TPU:1, one launch (start us, length us, event | category | flops | bytes accessed | tf_op | source)
XLA Modules:
  0.0 111.0 jit_solution(13305406758415592225)
XLA Ops:
  0.6 107.7 %shard_map.110 = (bf16[8,256,128]{2,1,0:T(8,128)(2,1)}, bf16[8,256,128]{2,1,0:T(8,128)(2,1)}, f32[2,128,640]{2,1,0:T(8,128)}, f32[2,128,128]{2,1,0:T(8,128)}, f32[1,128]{1,0:T(1,128)}) custom-call(bf16[8,256,128]{2,1,0:T(8,128)(2,1)} %bitcast.6, s32[1,256]{1,0:T(1,128)} %mask_in.1, s32[1,256]{1,0:T(1,128)} %chain_in.1, f32[1,128]{1,0:T(1,128)} %bitcast.8, ...), custom_call_target="tpu_custom_call" | custom-call | tf_op jit(solution)/shard_map/pallas_call | solution.py:646
  108.3 2.5 %shard_map.111 = (bf16[8,256,128]{2,1,0:T(8,128)(2,1)}, bf16[8,256,128]{2,1,0:T(8,128)(2,1)}, f32[2,128,640]{2,1,0:T(8,128)}, f32[2,128,128]{2,1,0:T(8,128)}, f32[1,128]{1,0:T(1,128)}) custom-call(bf16[8,256,128]{2,1,0:T(8,128)(2,1)} %get-tuple-element.15.refs_0_, bf16[8,256,128]{2,1,0:T(8,128)(2,1)} %get-tuple-element.16.refs_1_, ...), custom_call_target="tpu_custom_call" | custom-call | tf_op jit(solution)/shard_map/pallas_call | solution.py:660

commit v5 on v4

--- a/solution.py
+++ b/solution.py
@@ -499,13 +499,17 @@
             chain_s[...] += grad.astype(F32) * sc_s[pl.ds(q, 1), :]
 
         loop(finish, p)
+        if p == 0:
+            bulk(rf_s, n - 1, 3).wait_recv()
+            xf_s[...] = summed(rf_s, n)
+            across(xf_s, yf_s, 4)
     column_sum = jnp.sum(chain_s[...], axis=1, keepdims=True)
     cg_s[...] = jnp.sum(diag * column_sum, axis=0, keepdims=True)
     cr_s[me] = cg_s[...]
     spread(cg_s, cr_s, 6)
-    bulk(rf_s, n - 1, 3).wait_recv()
-    xf_s[...] = summed(rf_s, n)
-    across(xf_s, yf_s, 4)
+    bulk(yf_s, dp - 1, 4).wait_recv()
+    af_s[me] = (summed(yf_s, dp) * inverse).astype(BF16)
+    spread(af_s.at[me], af_s, 5)
     for p in range(2):
         def write_grad(i, q):
             pgv_s[i, p * half:(p + 1) * half, :] = nt(eye_s[0:half, 0:half], dz_s[1, q]).astype(BF16)
@@ -516,9 +520,6 @@
     bulk(cr_s, n - 1, 6).wait_recv()
     cx_s[...] = summed(cr_s, n)
     across(cx_s, cy_s, 7)
-    bulk(yf_s, dp - 1, 4).wait_recv()
-    af_s[me] = (summed(yf_s, dp) * inverse).astype(BF16)
-    spread(af_s.at[me], af_s, 5)
     bulk(ae_s, n - 1, 2).wait_recv()
     full = ae_s[...].reshape(8 * CH, CH).astype(F32)
     for b in range(5):

time: 111 us -> 112 us (level)
  no operation moved by 1% of the time
where the time goes in v5:
time: 112 us
  Pallas kernels  111 us (99%)
    pallas_call x1, Pallas kernels, body(): pl.pallas_call(functools.partial(kernel, n, dp), out_shape=shapes, in_spe...  109 us
    pallas_call x1, Pallas kernels, body(): pl.pallas_call(hand_over, out_shape=shapes, in_specs=[anywhere] * 5, out_...  2.49 us

profile of v5, /device:TPU:1, one launch (start us, length us, event | category | flops | bytes accessed | tf_op | source)
XLA Modules:
  0.0 112.1 jit_solution(8351844666661869745)
XLA Ops:
  0.6 108.8 %shard_map.110 = (bf16[8,256,128]{2,1,0:T(8,128)(2,1)}, bf16[8,256,128]{2,1,0:T(8,128)(2,1)}, f32[2,128,640]{2,1,0:T(8,128)}, f32[2,128,128]{2,1,0:T(8,128)}, f32[1,128]{1,0:T(1,128)}) custom-call(bf16[8,256,128]{2,1,0:T(8,128)(2,1)} %bitcast.6, s32[1,256]{1,0:T(1,128)} %mask_in.1, s32[1,256]{1,0:T(1,128)} %chain_in.1, f32[1,128]{1,0:T(1,128)} %bitcast.8, ...), custom_call_target="tpu_custom_call" | custom-call | tf_op jit(solution)/shard_map/pallas_call | solution.py:647
  109.4 2.5 %shard_map.111 = (bf16[8,256,128]{2,1,0:T(8,128)(2,1)}, bf16[8,256,128]{2,1,0:T(8,128)(2,1)}, f32[2,128,640]{2,1,0:T(8,128)}, f32[2,128,128]{2,1,0:T(8,128)}, f32[1,128]{1,0:T(1,128)}) custom-call(bf16[8,256,128]{2,1,0:T(8,128)(2,1)} %get-tuple-element.15.refs_0_, bf16[8,256,128]{2,1,0:T(8,128)(2,1)} %get-tuple-element.16.refs_1_, ...), custom_call_target="tpu_custom_call" | custom-call | tf_op jit(solution)/shard_map/pallas_call | solution.py:661
